TPU v7x, 512 devices: a whole 4x4x16 slice. The times are simulated.
512 devices in a mesh: row: 16 (over y, x), col: 32 (over z, core).
Axes of the slice: x: 4, y: 4, z: 16, core: 2. Of those that a mesh axis runs over, the one named last changes fastest.
Arguments:
- tokens: bfloat16 [512, 8192], P('col', 'row'), may hold values from -6 to 6
- w_gate: bfloat16 [8192, 16384], P('row', 'col'), may hold values from -0.0625 to 0.0625
- w_up: bfloat16 [8192, 16384], P('row', 'col'), may hold values from -0.0625 to 0.0625
- w_down: bfloat16 [16384, 8192], P('col', 'row'), may hold values from -0.046875 to 0.046875
- upstream: bfloat16 [512, 8192], P('col', 'row'), may hold values from -3 to 3
Outputs:
- grad_tokens: bfloat16 [512, 8192], P('col', 'row')
- grad_gate: bfloat16 [8192, 16384], P('row', 'col')
- grad_up: bfloat16 [8192, 16384], P('row', 'col')
- grad_down: bfloat16 [16384, 8192], P('col', 'row')
All inputs are finite; a program needn't handle non-finite values.
Results may differ from a plain program's by a relative error of at most 0.0049.
Values may be sent and summed in bfloat16 or wider, within the bound.
A program may use at most 64 MiB of HBM per device.

v0:
```python
import jax
import jax.numpy as jnp
from jax import lax
from jax.sharding import PartitionSpec as P


def forward_hidden(gate_sum, up_sum):
    logistic = jax.nn.sigmoid(gate_sum)
    return (gate_sum * logistic * up_sum).astype(jnp.bfloat16)


def backward_gates(gate_sum, up_sum, slope_sum):
    logistic = jax.nn.sigmoid(gate_sum)
    activated = gate_sum * logistic
    grad_gate_act = (slope_sum * up_sum * logistic * (1.0 + gate_sum * (1.0 - logistic))).astype(
        jnp.bfloat16
    )
    grad_up_act = (slope_sum * activated).astype(jnp.bfloat16)
    return (grad_gate_act, grad_up_act)


def contract_last(left, right):
    return lax.dot_general(
        left, right, (((1,), (1,)), ((), ())), preferred_element_type=jnp.float32
    )


def contract_first(left, right):
    return lax.dot_general(
        left, right, (((0,), (0,)), ((), ())), preferred_element_type=jnp.float32
    )


def body(tokens, w_gate, w_up, w_down, upstream):
    tokens_all, upstream_all = (
        lax.all_gather(tokens, "col", axis=0, tiled=True),
        lax.all_gather(upstream, "col", axis=0, tiled=True),
    )
    gate_part = jnp.dot(tokens_all, w_gate, preferred_element_type=jnp.float32)
    up_part = jnp.dot(tokens_all, w_up, preferred_element_type=jnp.float32)
    slope_part = contract_last(upstream_all, w_down)
    gate_piece, up_piece = (
        lax.psum_scatter(gate_part, "row", scatter_dimension=0, tiled=True),
        lax.psum_scatter(up_part, "row", scatter_dimension=0, tiled=True),
    )
    hidden_piece = forward_hidden(gate_piece, up_piece)
    hidden_all = lax.all_gather(hidden_piece, "row", axis=0, tiled=True)
    slope_piece = lax.psum_scatter(slope_part, "row", scatter_dimension=0, tiled=True)
    gate_grad_piece, up_grad_piece = backward_gates(gate_piece, up_piece, slope_piece)
    grad_gate_all, grad_up_all = (
        lax.all_gather(gate_grad_piece, "row", axis=0, tiled=True),
        lax.all_gather(up_grad_piece, "row", axis=0, tiled=True),
    )
    grad_down = contract_first(hidden_all, upstream_all).astype(jnp.bfloat16)
    grad_gate = contract_first(tokens_all, grad_gate_all).astype(jnp.bfloat16)
    grad_up = contract_first(tokens_all, grad_up_all).astype(jnp.bfloat16)
    input_part = contract_last(grad_gate_all, w_gate) + contract_last(grad_up_all, w_up)
    grad_tokens = lax.psum_scatter(input_part, "col", scatter_dimension=0, tiled=True).astype(
        jnp.bfloat16
    )
    return (grad_tokens, grad_gate, grad_up, grad_down)


def solution(mesh):
    return jax.shard_map(
        body,
        mesh=mesh,
        in_specs=(
            P("col", "row"),
            P("row", "col"),
            P("row", "col"),
            P("col", "row"),
            P("col", "row"),
        ),
        out_specs=(P("col", "row"), P("row", "col"), P("row", "col"), P("col", "row")),
        check_vma=False,
    )
```

profile of v0, /device:TPU:1, one launch (start us, length us, event | category | flops | bytes accessed | tf_op | source)
XLA Modules:
  0.0 477.1 jit_solution(12661166016115095918)
XLA Ops:
  7.2 0.0 copy-start
  7.2 0.0 reduce-scatter.7.cloned.1.call-start
  7.2 39.4 %all_gather.16 = bf16[512,512]{1,0:T(8,128)(2,1)S(1)} all-gather(bf16[16,512]{1,0:T(8,128)(2,1)} %param.5), channel_id=1, replica_groups=mesh['row'=16,'col'=32] {'col'}, dimensions={0}, use_global_device_ids=true | all-gather | bytes 540672 | tf_op jit(solution)/shard_map/all_gather | solution.py:36
  46.6 1.4 fusion.4
  48.0 0.0 reduce-scatter.7.cloned.1.call-update
  48.1 0.0 reduce-scatter.9.cloned.1.call-start
  48.1 1.5 fusion.5
  49.6 0.0 reduce-scatter.9.cloned.1.call-update
  49.6 0.0 copy-start.2
  49.6 0.0 reduce-scatter.5.cloned.1.call-start
  49.7 0.6 copy-done.3
  50.3 28.5 %all_gather.15 = bf16[512,512]{1,0:T(8,128)(2,1)S(1)} all-gather(bf16[16,512]{1,0:T(8,128)(2,1)S(1)} %copy-done.3), channel_id=1, replica_groups=mesh['row'=16,'col'=32] {'col'}, dimensions={0}, use_global_device_ids=true | all-gather | bytes 540672 | tf_op jit(solution)/shard_map/all_gather | solution.py:37
  78.8 1.5 fusion.3
  80.3 0.0 reduce-scatter.5.cloned.1.call-update
  80.3 0.0 reduce-scatter.11.cloned.1.call-start
  80.3 50.0 %reduce-scatter.7.cloned.1.call-done = f32[32,512]{1,0:T(8,128)} async-done(((f32[512,512]{1,0:T(8,128)}), f32[32,512]{1,0:T(8,128)}) %reduce-scatter.7.cloned.1.call-update) | async-done | bytes 65552 | tf_op jit(solution)/shard_map/reduce_scatter | solution.py:44
  130.4 92.4 %reduce-scatter.9.cloned.1.call-done = f32[32,512]{1,0:T(8,128)} async-done(((f32[512,512]{1,0:T(8,128)}), f32[32,512]{1,0:T(8,128)}) %reduce-scatter.9.cloned.1.call-update) | async-done | bytes 65552 | tf_op jit(solution)/shard_map/reduce_scatter | solution.py:43
  222.7 91.8 %reduce-scatter.5.cloned.1.call-done = f32[32,512]{1,0:T(8,128)} async-done(((f32[512,512]{1,0:T(8,128)}), f32[32,512]{1,0:T(8,128)}) %reduce-scatter.5.cloned.1.call-update) | async-done | bytes 65552 | tf_op jit(solution)/shard_map/reduce_scatter | solution.py:48
  314.5 0.9 multiply_convert_fusion
  315.5 17.5 %all_gather.17 = bf16[512,512]{1,0:T(8,128)(2,1)S(1)} all-gather(bf16[32,512]{1,0:T(8,128)(2,1)S(1)} %get-tuple-element.9), channel_id=1, replica_groups=mesh['row'=16,'col'=32] {'row'}, dimensions={0}, use_global_device_ids=true | all-gather | bytes 557056 | tf_op jit(solution)/shard_map/all_gather | solution.py:51
  333.0 0.5 fusion.6
  333.4 17.0 %all_gather.18 = bf16[512,512]{1,0:T(8,128)(2,1)S(1)} all-gather(bf16[32,512]{1,0:T(8,128)(2,1)S(1)} %get-tuple-element.10), channel_id=1, replica_groups=mesh['row'=16,'col'=32] {'row'}, dimensions={0}, use_global_device_ids=true | all-gather | bytes 557056 | tf_op jit(solution)/shard_map/all_gather | solution.py:52
  350.4 1.4 convolution_add_fusion
  351.8 0.0 reduce-scatter.11.cloned.1.call-update
  351.9 0.5 fusion.1
  352.3 1.0 copy.10
  353.3 0.5 fusion
  353.8 1.0 copy.9
  354.8 17.6 %all_gather.19 = bf16[512,512]{1,0:T(8,128)(2,1)S(1)} all-gather(bf16[32,512]{1,0:T(8,128)(2,1)S(1)} %get-tuple-element.8), channel_id=1, replica_groups=mesh['row'=16,'col'=32] {'row'}, dimensions={0}, use_global_device_ids=true | all-gather | bytes 557056 | tf_op jit(solution)/shard_map/all_gather | solution.py:47
  372.5 1.3 convolution_convert_fusion
  373.7 95.5 %reduce-scatter.11.cloned.1.call-done = f32[16,512]{1,0:T(8,128)} async-done(((f32[512,512]{1,0:T(8,128)}), f32[16,512]{1,0:T(8,128)}) %reduce-scatter.11.cloned.1.call-update) | async-done | bytes 32784 | tf_op jit(solution)/shard_map/reduce_scatter | solution.py:58
  469.2 1.4 convert_element_type.29
  (5 shorter events, 0.0 us)
Async XLA Ops:
  7.2 41.0 %copy-start = (bf16[512,512]{1,0:T(8,128)(2,1)S(1)}, bf16[512,512]{1,0:T(8,128)(2,1)}, u32[]{:S(2)}) copy-start(bf16[512,512]{1,0:T(8,128)(2,1)} %param.6) | copy-start | bytes 1572868
  7.2 39.4 %copy-start.1 = (bf16[512,512]{1,0:T(8,128)(2,1)S(1)}, bf16[512,512]{1,0:T(8,128)(2,1)}, u32[]{:S(2)}) copy-start(bf16[512,512]{1,0:T(8,128)(2,1)} %param.7) | copy-start | bytes 1572868
  7.2 123.2 %reduce-scatter.7.cloned.1.call-start = ((), (), s32[]{:S(2)}) async-start(), calls=%async_computation.5 | async-start | bytes 1114112 | tf_op jit(solution)/shard_map/reduce_scatter | solution.py:44
  48.1 174.7 %reduce-scatter.9.cloned.1.call-start = ((), (), s32[]{:S(2)}) async-start(), calls=%async_computation.6 | async-start | bytes 1114112 | tf_op jit(solution)/shard_map/reduce_scatter | solution.py:43
  49.6 0.7 copy-start.3
  49.6 29.2 %copy-start.2 = (bf16[512,512]{1,0:T(8,128)(2,1)S(1)}, bf16[512,512]{1,0:T(8,128)(2,1)}, u32[]{:S(2)}) copy-start(bf16[512,512]{1,0:T(8,128)(2,1)} %param.8) | copy-start | bytes 1572868
  49.6 264.9 %reduce-scatter.5.cloned.1.call-start = ((), (), s32[]{:S(2)}) async-start(), calls=%async_computation.4 | async-start | bytes 1114112 | tf_op jit(solution)/shard_map/reduce_scatter | solution.py:48
  80.3 388.9 %reduce-scatter.11.cloned.1.call-start = ((), (), s32[]{:S(2)}) async-start(), calls=%async_computation.7 | async-start | bytes 1081344 | tf_op jit(solution)/shard_map/reduce_scatter | solution.py:58
Sparse Core Ops, SparseCore 0:
  48.2 82.1 reduce-scatter.6
  135.0 87.6 reduce-scatter.8
  226.8 87.6 reduce-scatter.4
  352.0 117.1 reduce-scatter.10
where the time goes:
time: 479 us; the launch traced here: 477 us
  waiting for transfers between devices  330 us (69%)
  blocking collectives  120 us (25%)
  between operations  13.8 us (3%)
  matrix products  8.43 us (2%)
    reduce_scatter x1, waiting for transfers between devices, body(): lax.psum_scatter(input_part, 'col', scatter_dimension=0, tiled=True)  95.5 us
    reduce_scatter x1, waiting for transfers between devices, body(): lax.psum_scatter(gate_part, 'row', scatter_dimension=0, tiled=True)  92.4 us
    reduce_scatter x1, waiting for transfers between devices, body(): lax.psum_scatter(slope_part, 'row', scatter_dimension=0, tiled=True)  91.8 us
    reduce_scatter x1, waiting for transfers between devices, body(): lax.psum_scatter(up_part, 'row', scatter_dimension=0, tiled=True)  50 us
    all_gather x1, blocking collectives, body(): lax.all_gather(tokens, 'col', axis=0, tiled=True)  39.4 us
    all_gather x1, blocking collectives, body(): lax.all_gather(upstream, 'col', axis=0, tiled=True)  28.5 us
    all_gather x1, blocking collectives, body(): hidden_all = lax.all_gather(hidden_piece, 'row', axis=0, tiled=True)  17.6 us
    all_gather x1, blocking collectives, body(): lax.all_gather(gate_grad_piece, 'row', axis=0, tiled=True)  17.5 us
  transfers between devices with their start and end apart: 4, of which 4 were waited for; matrix products, arithmetic and copies ran while one was open for 1% of the time, Pallas kernels for 0%

commit v1 on v0

v1 whole, which is shorter than its diff:
```python
import jax
import jax.numpy as jnp
from jax import lax
from jax.experimental import pallas as pl
from jax.experimental.pallas import tpu as pltpu
from jax.sharding import PartitionSpec as P

MESH = pl.DeviceIdType.MESH
NX, NY, NZ = 4, 4, 16
CHUNKS = 4
ROWS = 128
B = 16
ORDER = [0, 1, -1, 2, -2, 3, -3, 4, -4, 5, -5, 6, -6, 7, -7, 8]
SLOT = {r: s for s, r in enumerate(ORDER)}
SLOT[-8] = SLOT[8]


def contract_last(left, right):
    return lax.dot_general(
        left, right, (((1,), (1,)), ((), ())), preferred_element_type=jnp.float32
    )


def contract_first(left, right):
    return lax.dot_general(
        left, right, (((0,), (0,)), ((), ())), preferred_element_type=jnp.float32
    )


def kernel(
    tokens_ref, wg_ref, wu_ref, wd_ref, upstream_ref,
    gt_ref, gg_ref, gu_ref, gd_ref,
    acts, weights, part, part16, got1, sum1, got2, hidden, inp, inp_got, inp16, inp_all, grads, gt_buf,
    in_sem, out_sem, a_send, a_recv, k_send, k_recv, b1_send, b1_recv, b2_send, b2_recv,
    c1_send, c1_recv, c2_send, c2_recv, e_send, e_recv, d_send, d_recv,
):
    row, col = lax.axis_index("row"), lax.axis_index("col")
    x, y = lax.rem(row, NX), lax.div(row, NX)
    z, core = lax.div(col, 2), lax.rem(col, 2)

    def along_x(d):
        return (y * NX + lax.rem(x + d, NX), col)

    def along_y(d):
        return (lax.rem(y + d, NY) * NX + x, col)

    def along_z(d):
        return (row, lax.rem(z + d % NZ, NZ) * 2 + core)

    sibling = (row, z * 2 + 1 - core)

    halves = ((along_x, x, along_y, y), (along_y, y, along_x, x))

    def put(src, dst, send, recv, peer):
        pltpu.make_async_remote_copy(
            src, dst, send, recv, device_id=peer, device_id_type=MESH
        ).start()

    def take(ref, sem):
        pltpu.make_async_copy(ref, ref, sem).wait()

    def shard(slot, c):
        return acts.at[:, pl.ds(pl.multiple_of(slot * 2 * B + c * B, B), B), :]

    mine = pl.ds(pl.multiple_of(core * B, B), B)
    loads = [
        pltpu.make_async_copy(tokens_ref, acts.at[0, mine, :], in_sem.at[0]),
        pltpu.make_async_copy(upstream_ref, acts.at[1, mine, :], in_sem.at[1]),
        pltpu.make_async_copy(wg_ref, weights.at[0], in_sem.at[2]),
        pltpu.make_async_copy(wu_ref, weights.at[1], in_sem.at[3]),
        pltpu.make_async_copy(wd_ref, weights.at[2], in_sem.at[4]),
    ]
    for load in loads:
        load.start()

    barrier = pltpu.get_barrier_semaphore()
    greet = [along_z(d) for d in (1, -1, 2, -2)] + [sibling]
    greet += [along_x(d) for d in (1, 2, 3)] + [along_y(d) for d in (1, 2, 3)]
    for peer in greet:
        pl.semaphore_signal(barrier, inc=1, device_id=peer, device_id_type=MESH)
    loads[0].wait()
    loads[1].wait()
    pl.semaphore_wait(barrier, len(greet))

    def gather_send(s):
        for sign in (1, -1):
            have = SLOT[-sign * 2 * s]
            for hop in (1, 2):
                rel = -sign * (2 * s + hop)
                if rel == 8:
                    continue
                put(
                    shard(have, core), shard(SLOT[rel], core), a_send.at[s], a_recv.at[s], along_z(sign * hop)
                )

    def gather_count(s):
        return 3 if s == 3 else 4

    def gather_take(s):
        n = gather_count(s)
        take(acts.at[:, 0 : n * B, :], a_recv.at[s])
        if s + 1 < 4:
            gather_send(s + 1)
        for rel in (2 * s + 1, -(2 * s + 1), 2 * s + 2, -(2 * s + 2)):
            if rel != -8:
                slot = SLOT[rel]
                put(shard(slot, core), shard(slot, core), k_send.at[s], k_recv.at[s], sibling)

    def project(c):
        rows = slice(c * ROWS, (c + 1) * ROWS)
        tok, ups = acts[0, rows, :], acts[1, rows, :]
        for i in range(3):
            if i < 2:
                p = jnp.dot(tok, weights[i], preferred_element_type=jnp.float32)
            else:
                p = contract_last(ups, weights[2])
            part[c, i] = p
            part16[c, i] = p.astype(jnp.bfloat16)
        for h, (first, at, _, _) in enumerate(halves):
            for d in (1, 2, 3):
                b = lax.rem(at + d, 4)
                block = pl.ds(pl.multiple_of(h * 64 + b * B, B), B)
                put(
                    part16.at[c, :, block, :], got1.at[c, h, d - 1], b1_send.at[c], b1_recv.at[c], first(d)
                )

    def add_first(c):
        take(got1.at[c], b1_recv.at[c])
        for h, (_, at, second, place) in enumerate(halves):
            block = pl.ds(pl.multiple_of(h * 64 + at * B, B), B)
            total = part[c, :, block, :]
            for d in range(3):
                total = total + got1[c, h, d].astype(jnp.float32)
            sum1[c, h] = total
            for d in (1, 2, 3):
                j = lax.rem(place + d, 4)
                cols = pl.ds(pl.multiple_of(j * 128, 128), 128)
                put(
                    sum1.at[c, h, :, :, cols], got2.at[c, h, d - 1], b2_send.at[c], b2_recv.at[c], second(d)
                )

    def own(c, h, at, place):
        rows = pl.ds(pl.multiple_of(c * ROWS + h * 64 + at * B, B), B)
        cols = pl.ds(pl.multiple_of(place * 128, 128), 128)
        return rows, cols

    def activate(c):
        take(got2.at[c], b2_recv.at[c])
        for h, (_, at, second, place) in enumerate(halves):
            rows, cols = own(c, h, at, place)
            total = sum1[c, h, :, :, cols]
            for d in range(3):
                total = total + got2[c, h, d]
            gate, up, slope = total[0], total[1], total[2]
            s = 1.0 / (1.0 + jnp.exp(-gate))
            activated = gate * s
            hidden[0, rows, cols] = (activated * up).astype(jnp.bfloat16)
            hidden[1, rows, cols] = (slope * up * s * (1.0 + gate * (1.0 - s))).astype(jnp.bfloat16)
            hidden[2, rows, cols] = (slope * activated).astype(jnp.bfloat16)
            block = hidden.at[:, rows, cols]
            for d in (1, 2, 3):
                put(block, block, c1_send.at[c], c1_recv.at[c], second(d))

    def spread(c):
        take(hidden.at[:, 0:96, 0:128], c1_recv.at[c])
        for h, (first, at, _, place) in enumerate(halves):
            rows, _ = own(c, h, at, place)
            block = hidden.at[:, rows, :]
            for d in (1, 2, 3):
                put(block, block, c2_send.at[c], c2_recv.at[c], first(d))

    def input_part(c):
        take(hidden.at[:, 0:96, :], c2_recv.at[c])
        rows = slice(c * ROWS, (c + 1) * ROWS)
        p = contract_last(hidden[1, rows, :], weights[0]) + contract_last(hidden[2, rows, :], weights[1])
        inp[c] = p.reshape(4, 2, B, 512)
        put(inp.at[c, :, 1 - core], inp_got.at[c], e_send.at[c], e_recv.at[c], sibling)

    def input_send(c):
        take(inp_got.at[c], e_recv.at[c])
        for i in range(4):
            slot = 4 * c + i
            total = inp[c, i, core] + inp_got[c, i]
            if slot == 0:
                inp_got[c, i] = total
            else:
                inp16[c, i] = total.astype(jnp.bfloat16)
                put(inp16.at[c, i], inp_all.at[slot - 1], d_send.at[0], d_recv.at[0], along_z(ORDER[slot]))

    def weight_grads():
        stores = []
        pairs = ((acts, 0, hidden, 1, gg_ref), (acts, 0, hidden, 2, gu_ref), (hidden, 0, acts, 1, gd_ref))
        for i, (left, li, right, ri, out) in enumerate(pairs):
            grads[i] = contract_first(left[li], right[ri]).astype(jnp.bfloat16)
            stores.append(pltpu.make_async_copy(grads.at[i], out, out_sem.at[i]))
            stores[-1].start()
        return stores

    def ready(c):
        if c == 0:
            shard0 = shard(0, core)
            put(shard0, shard0, k_send.at[4], k_recv.at[4], sibling)
            gather_send(0)
            gather_take(0)
            take(acts.at[:, 0:B, :], k_recv.at[4])
        n = gather_count(c)
        take(acts.at[:, 0 : n * B, :], k_recv.at[c])

    ready(0)
    for load in loads[2:]:
        load.wait()
    project(0)
    gather_take(1)
    ready(1)
    project(1)
    add_first(0)
    gather_take(2)
    ready(2)
    project(2)
    activate(0)
    add_first(1)
    gather_take(3)
    ready(3)
    project(3)
    spread(0)
    activate(1)
    add_first(2)
    input_part(0)
    spread(1)
    activate(2)
    add_first(3)
    input_send(0)
    input_part(1)
    spread(2)
    activate(3)
    input_send(1)
    input_part(2)
    spread(3)
    input_send(2)
    input_part(3)
    input_send(3)
    stores = weight_grads()

    take(inp_all, d_recv.at[0])
    total = inp_got[0, 0]
    for i in range(15):
        total = total + inp_all[i].astype(jnp.float32)
    gt_buf[...] = total.astype(jnp.bfloat16)
    stores.append(pltpu.make_async_copy(gt_buf, gt_ref, out_sem.at[3]))
    stores[-1].start()

    for s in range(4):
        n = gather_count(s)
        take(acts.at[:, 0 : n * B, :], a_send.at[s])
        take(acts.at[:, 0 : n * B, :], k_send.at[s])
    take(acts.at[:, 0:B, :], k_send.at[4])
    for c in range(CHUNKS):
        take(got1.at[c], b1_send.at[c])
        take(got2.at[c], b2_send.at[c])
        take(hidden.at[:, 0:96, 0:128], c1_send.at[c])
        take(hidden.at[:, 0:96, :], c2_send.at[c])
        take(inp_got.at[c], e_send.at[c])
    take(inp_all, d_send.at[0])
    for store in stores:
        store.wait()


def body(tokens, w_gate, w_up, w_down, upstream):
    bf16, f32 = jnp.bfloat16, jnp.float32
    sem = pltpu.SemaphoreType.DMA
    out = lambda *shape: jax.ShapeDtypeStruct(shape, bf16)
    return pl.pallas_call(
        kernel,
        name="mlp",
        out_shape=(out(16, 512), out(512, 512), out(512, 512), out(512, 512)),
        in_specs=[pl.BlockSpec(memory_space=pltpu.HBM)] * 5,
        out_specs=(pl.BlockSpec(memory_space=pltpu.HBM),) * 4,
        scratch_shapes=[
            pltpu.VMEM((2, 512, 512), bf16),
            pltpu.VMEM((3, 512, 512), bf16),
            pltpu.VMEM((CHUNKS, 3, ROWS, 512), f32),
            pltpu.VMEM((CHUNKS, 3, ROWS, 512), bf16),
            pltpu.VMEM((CHUNKS, 2, 3, 3, B, 512), bf16),
            pltpu.VMEM((CHUNKS, 2, 3, B, 512), f32),
            pltpu.VMEM((CHUNKS, 2, 3, 3, B, 128), f32),
            pltpu.VMEM((3, 512, 512), bf16),
            pltpu.VMEM((CHUNKS, 4, 2, B, 512), f32),
            pltpu.VMEM((CHUNKS, 4, B, 512), f32),
            pltpu.VMEM((CHUNKS, 4, B, 512), bf16),
            pltpu.VMEM((15, B, 512), bf16),
            pltpu.VMEM((3, 512, 512), bf16),
            pltpu.VMEM((B, 512), bf16),
            sem((5,)), sem((4,)),
            sem((4,)), sem((4,)), sem((5,)), sem((5,)),
            sem((4,)), sem((4,)), sem((4,)), sem((4,)),
            sem((4,)), sem((4,)), sem((4,)), sem((4,)),
            sem((4,)), sem((4,)), sem((1,)), sem((1,)),
        ],
        compiler_params=pltpu.CompilerParams(
            collective_id=0, has_side_effects=True, vmem_limit_bytes=60 << 20
        ),
        cost_estimate=pl.CostEstimate(flops=2 << 30, bytes_accessed=4 << 20, transcendentals=0),
    )(tokens, w_gate, w_up, w_down, upstream)


def solution(mesh):
    return jax.shard_map(
        body,
        mesh=mesh,
        in_specs=(P("col", "row"), P("row", "col"), P("row", "col"), P("col", "row"), P("col", "row")),
        out_specs=(P("col", "row"), P("row", "col"), P("row", "col"), P("col", "row")),
        check_vma=False,
    )
```

time: 479 us -> 76.1 us (0.16)
  waiting for transfers between devices: 330 us -> 0 us
  blocking collectives: 120 us -> 0 us
  Pallas kernels: 0 us -> 69.5 us
  between operations: 13.8 us -> 0.64 us
  matrix products: 8.43 us -> 0 us
    reduce_scatter x4 -> x0, waiting for transfers between devices: 330 us -> none  [the longest x1 95.5 us: body(): lax.psum_scatter(input_part, 'col', scatter_dimension=0, tiled=True)]
    all_gather x5 -> x0, blocking collectives: 120 us -> none  [the longest x1 39.4 us: body(): lax.all_gather(tokens, 'col', axis=0, tiled=True)]
    pallas_call x0 -> x1, Pallas kernels: none -> 69.5 us  [body(): pl.pallas_call(kernel, name='mlp', out_shape=(out(16, 512), out(512, 512)...]
    dot_general x8 -> x0, matrix products: 8.43 us -> none  [the longest x3 3.37 us: contract_last(): lax.dot_general(left, right, (((1,), (1,)), ((), ())), preferred_element_...]
  transfers between devices with their start and end apart: 4 -> 0, of which waited for: 4 -> 0; matrix products, arithmetic and copies ran while one was open for 1% -> 0% of each run, Pallas kernels for 0% -> 0%
where the time goes in v1:
time: 76.1 us; the launch traced here: 75.4 us
  Pallas kernels  69.5 us (91%)
  local copies, waits for them, and re-layouts  5.28 us (7%)
    pallas_call x1, Pallas kernels, body(): pl.pallas_call(kernel, name='mlp', out_shape=(out(16, 512), out(512, 512)...  69.5 us
    unnamed x8, local copies, waits for them, and re-layouts  5.28 us

profile of v1, /device:TPU:1, one launch (start us, length us, event | category | flops | bytes accessed | tf_op | source)
XLA Modules:
  0.0 75.4 jit_solution(10194757957610107869)
XLA Ops:
  0.6 69.5 %mlp.1 = (bf16[16,512]{1,0:T(8,128)(2,1)}, bf16[512,512]{1,0:T(8,128)(2,1)}, bf16[512,512]{1,0:T(8,128)(2,1)}, bf16[512,512]{1,0:T(8,128)(2,1)}) custom-call(bf16[16,512]{1,0:T(8,128)(2,1)} %tokens_ref.1, bf16[512,512]{1,0:T(8,128)(2,1)} %wg_ref.1, bf16[512,512]{1,0:T(8,128)(2,1)} %wu_ref.1, bf16[512,512]{1,0:T(8,128)(2,1)} %wd_ref.1, ...), custom_call_target="tpu_custom_call" | custom-call | flops 2147483648 | bytes 4194304 | tf_op jit(solution)/shard_map/mlp/pallas_call | solution.py:272
  70.1 1.3 %copy.13 = bf16[16,512]{1,0:T(8,128)(2,1)} copy(bf16[16,512]{1,0:T(8,128)(2,1)} %get-tuple-element.8) | data formatting | bytes 32768
  71.4 0.0 copy-start.1
  71.4 1.9 %copy.14 = bf16[512,512]{1,0:T(8,128)(2,1)} copy(bf16[512,512]{1,0:T(8,128)(2,1)} %get-tuple-element.9) | data formatting | bytes 1048576
  73.3 0.0 copy-done.1
  73.3 0.0 copy-start
  73.4 0.8 %copy.15 = bf16[512,512]{1,0:T(8,128)(2,1)} copy(bf16[512,512]{1,0:T(8,128)(2,1)S(1)} %copy-done.1) | data formatting | bytes 1048576
  74.1 0.4 copy-done
  74.6 0.8 %copy.16 = bf16[512,512]{1,0:T(8,128)(2,1)} copy(bf16[512,512]{1,0:T(8,128)(2,1)S(1)} %copy-done) | data formatting | bytes 1048576
Async XLA Ops:
  71.4 1.9 %copy-start.1 = (bf16[512,512]{1,0:T(8,128)(2,1)S(1)}, bf16[512,512]{1,0:T(8,128)(2,1)}, u32[]{:S(2)}) copy-start(bf16[512,512]{1,0:T(8,128)(2,1)} %get-tuple-element.10) | copy-start | bytes 1572868
  73.3 1.2 %copy-start = (bf16[512,512]{1,0:T(8,128)(2,1)S(1)}, bf16[512,512]{1,0:T(8,128)(2,1)}, u32[]{:S(2)}) copy-start(bf16[512,512]{1,0:T(8,128)(2,1)} %get-tuple-element.11) | copy-start | bytes 1572868

commit v2 on v1

--- a/solution.py
+++ b/solution.py
@@ -13,6 +13,42 @@
 ORDER = [0, 1, -1, 2, -2, 3, -3, 4, -4, 5, -5, 6, -6, 7, -7, 8]
 SLOT = {r: s for s, r in enumerate(ORDER)}
 SLOT[-8] = SLOT[8]
+REACH = (3, 3, 2)
+BASE = [sum(REACH[:s]) for s in range(len(REACH) + 1)]
+STAGES = len(REACH)
+
+SCHEDULE = (
+    ("relay", 0),
+    ("nearer", 0),
+    ("project", 0),
+    ("relay", 1),
+    ("nearer", 1),
+    ("project", 2),
+    ("project", 1),
+    ("relay", 2),
+    ("nearer", 2),
+    ("add", 2),
+    ("project", 3),
+    ("activate", 2),
+    ("add", 1),
+    ("add", 3),
+    ("spread", 2),
+    ("activate", 3),
+    ("add", 0),
+    ("activate", 1),
+    ("product", 2),
+    ("spread", 3),
+    ("send", 2),
+    ("activate", 0),
+    ("product", 3),
+    ("spread", 1),
+    ("spread", 0),
+    ("send", 3),
+    ("product", 1),
+    ("send", 1),
+    ("product", 0),
+    ("send", 0),
+)
 
 
 def contract_last(left, right):
@@ -30,8 +66,8 @@
 def kernel(
     tokens_ref, wg_ref, wu_ref, wd_ref, upstream_ref,
     gt_ref, gg_ref, gu_ref, gd_ref,
-    acts, weights, part, part16, got1, sum1, got2, hidden, inp, inp_got, inp16, inp_all, grads, gt_buf,
-    in_sem, out_sem, a_send, a_recv, k_send, k_recv, b1_send, b1_recv, b2_send, b2_recv,
+    acts, weights, part, part16, got1, sum1, got2, hidden, inp, inp_got, inp16, inp_all,
+    in_sem, a_send, a_recv, k_send, k_recv, b1_send, b1_recv, b2_send, b2_recv,
     c1_send, c1_recv, c2_send, c2_recv, e_send, e_recv, d_send, d_recv,
 ):
     row, col = lax.axis_index("row"), lax.axis_index("col")
@@ -74,7 +110,7 @@
         load.start()
 
     barrier = pltpu.get_barrier_semaphore()
-    greet = [along_z(d) for d in (1, -1, 2, -2)] + [sibling]
+    greet = [along_z(sign * d) for d in range(1, max(REACH) + 1) for sign in (1, -1)] + [sibling]
     greet += [along_x(d) for d in (1, 2, 3)] + [along_y(d) for d in (1, 2, 3)]
     for peer in greet:
         pl.semaphore_signal(barrier, inc=1, device_id=peer, device_id_type=MESH)
@@ -82,31 +118,54 @@
     loads[1].wait()
     pl.semaphore_wait(barrier, len(greet))
 
+    def far(s):
+        return [r for r in (BASE[s + 1], -BASE[s + 1]) if r != -8]
+
+    def near(s):
+        return [sign * d for d in range(BASE[s] + 1, BASE[s + 1]) for sign in (1, -1)]
+
     def gather_send(s):
-        for sign in (1, -1):
-            have = SLOT[-sign * 2 * s]
-            for hop in (1, 2):
-                rel = -sign * (2 * s + hop)
+        for hop in range(REACH[s], 0, -1):
+            for sign in (1, -1):
+                have, rel = -sign * BASE[s], -sign * (BASE[s] + hop)
+                if rel == 8:
+                    rel = -8 if sign > 0 else 8
                 if rel == 8:
                     continue
+                relay = 2 * s + int(hop == REACH[s])
                 put(
-                    shard(have, core), shard(SLOT[rel], core), a_send.at[s], a_recv.at[s], along_z(sign * hop)
+                    shard(SLOT[have], core), shard(SLOT[rel], core),
+                    a_send.at[relay], a_recv.at[relay], along_z(sign * hop),
                 )
 
-    def gather_count(s):
-        return 3 if s == 3 else 4
-
-    def gather_take(s):
-        n = gather_count(s)
-        take(acts.at[:, 0 : n * B, :], a_recv.at[s])
-        if s + 1 < 4:
+    def to_sibling(rels, sem):
+        for rel in rels:
+            put(shard(SLOT[rel], core), shard(SLOT[rel], core), k_send.at[sem], k_recv.at[sem], sibling)
+
+    def few(n):
+        return acts.at[:, 0 : n * B, :]
+
+    groups = [f(s) for s in range(STAGES) for f in (near, far)]
+
+    def relay(s):
+        take(few(len(far(s))), a_recv.at[2 * s + 1])
+        if s + 1 < STAGES:
             gather_send(s + 1)
-        for rel in (2 * s + 1, -(2 * s + 1), 2 * s + 2, -(2 * s + 2)):
-            if rel != -8:
-                slot = SLOT[rel]
-                put(shard(slot, core), shard(slot, core), k_send.at[s], k_recv.at[s], sibling)
+        to_sibling(far(s), 2 * s + 1)
+
+    def nearer(s):
+        if near(s):
+            take(few(len(near(s))), a_recv.at[2 * s])
+            to_sibling(near(s), 2 * s)
+
+    here = []
 
     def project(c):
+        for rel in ORDER[4 * c : 4 * c + 4]:
+            group = next((g for g, rels in enumerate(groups) if rel in rels), 2 * STAGES)
+            if group not in here:
+                here.append(group)
+                take(few(len(groups[group]) if rel else 1), k_recv.at[group])
         rows = slice(c * ROWS, (c + 1) * ROWS)
         tok, ups = acts[0, rows, :], acts[1, rows, :]
         for i in range(3):
@@ -188,72 +247,36 @@
                 put(inp16.at[c, i], inp_all.at[slot - 1], d_send.at[0], d_recv.at[0], along_z(ORDER[slot]))
 
     def weight_grads():
-        stores = []
         pairs = ((acts, 0, hidden, 1, gg_ref), (acts, 0, hidden, 2, gu_ref), (hidden, 0, acts, 1, gd_ref))
-        for i, (left, li, right, ri, out) in enumerate(pairs):
-            grads[i] = contract_first(left[li], right[ri]).astype(jnp.bfloat16)
-            stores.append(pltpu.make_async_copy(grads.at[i], out, out_sem.at[i]))
-            stores[-1].start()
-        return stores
-
-    def ready(c):
-        if c == 0:
-            shard0 = shard(0, core)
-            put(shard0, shard0, k_send.at[4], k_recv.at[4], sibling)
-            gather_send(0)
-            gather_take(0)
-            take(acts.at[:, 0:B, :], k_recv.at[4])
-        n = gather_count(c)
-        take(acts.at[:, 0 : n * B, :], k_recv.at[c])
-
-    ready(0)
-    for load in loads[2:]:
-        load.wait()
-    project(0)
-    gather_take(1)
-    ready(1)
-    project(1)
-    add_first(0)
-    gather_take(2)
-    ready(2)
-    project(2)
-    activate(0)
-    add_first(1)
-    gather_take(3)
-    ready(3)
-    project(3)
-    spread(0)
-    activate(1)
-    add_first(2)
-    input_part(0)
-    spread(1)
-    activate(2)
-    add_first(3)
-    input_send(0)
-    input_part(1)
-    spread(2)
-    activate(3)
-    input_send(1)
-    input_part(2)
-    spread(3)
-    input_send(2)
-    input_part(3)
-    input_send(3)
-    stores = weight_grads()
+        for left, li, right, ri, out in pairs:
+            out[...] = contract_first(left[li], right[ri]).astype(jnp.bfloat16)
+
+    gather_send(0)
+    to_sibling((0,), 2 * STAGES)
+    loaded = False
+    tasks = dict(
+        relay=relay, nearer=nearer, project=project, add=add_first, activate=activate, spread=spread,
+        product=input_part, send=input_send,
+    )
+    for name, c in SCHEDULE:
+        if name == "project" and not loaded:
+            for load in loads[2:]:
+                load.wait()
+            loaded = True
+        tasks[name](c)
+    weight_grads()
 
     take(inp_all, d_recv.at[0])
     total = inp_got[0, 0]
     for i in range(15):
         total = total + inp_all[i].astype(jnp.float32)
-    gt_buf[...] = total.astype(jnp.bfloat16)
-    stores.append(pltpu.make_async_copy(gt_buf, gt_ref, out_sem.at[3]))
-    stores[-1].start()
-
-    for s in range(4):
-        n = gather_count(s)
-        take(acts.at[:, 0 : n * B, :], a_send.at[s])
-        take(acts.at[:, 0 : n * B, :], k_send.at[s])
-    take(acts.at[:, 0:B, :], k_send.at[4])
+    gt_ref[...] = total.astype(jnp.bfloat16)
+
+    for group, rels in enumerate(groups):
+        if rels:
+            take(few(len(rels)), a_send.at[group])
+            take(few(len(rels)), k_send.at[group])
+    take(few(1), k_send.at[2 * STAGES])
     for c in range(CHUNKS):
         take(got1.at[c], b1_send.at[c])
         take(got2.at[c], b2_send.at[c])
@@ -261,20 +284,27 @@
         take(hidden.at[:, 0:96, :], c2_send.at[c])
         take(inp_got.at[c], e_send.at[c])
     take(inp_all, d_send.at[0])
-    for store in stores:
-        store.wait()
+
+
+def write_out(*refs):
+    sems = refs[8]
+    copies = [pltpu.make_async_copy(refs[i], refs[4 + i], sems.at[i]) for i in range(4)]
+    for copy in copies:
+        copy.start()
+    for copy in copies:
+        copy.wait()
 
 
 def body(tokens, w_gate, w_up, w_down, upstream):
     bf16, f32 = jnp.bfloat16, jnp.float32
     sem = pltpu.SemaphoreType.DMA
-    out = lambda *shape: jax.ShapeDtypeStruct(shape, bf16)
-    return pl.pallas_call(
+    shapes = ((16, 512), (512, 512), (512, 512), (512, 512))
+    results = pl.pallas_call(
         kernel,
         name="mlp",
-        out_shape=(out(16, 512), out(512, 512), out(512, 512), out(512, 512)),
+        out_shape=tuple(pltpu.VMEM(shape, bf16) for shape in shapes),
         in_specs=[pl.BlockSpec(memory_space=pltpu.HBM)] * 5,
-        out_specs=(pl.BlockSpec(memory_space=pltpu.HBM),) * 4,
+        out_specs=(pl.BlockSpec(memory_space=pltpu.VMEM),) * 4,
         scratch_shapes=[
             pltpu.VMEM((2, 512, 512), bf16),
             pltpu.VMEM((3, 512, 512), bf16),
@@ -288,10 +318,8 @@
             pltpu.VMEM((CHUNKS, 4, B, 512), f32),
             pltpu.VMEM((CHUNKS, 4, B, 512), bf16),
             pltpu.VMEM((15, B, 512), bf16),
-            pltpu.VMEM((3, 512, 512), bf16),
-            pltpu.VMEM((B, 512), bf16),
-            sem((5,)), sem((4,)),
-            sem((4,)), sem((4,)), sem((5,)), sem((5,)),
+            sem((5,)),
+            sem((2 * STAGES,)), sem((2 * STAGES,)), sem((2 * STAGES + 1,)), sem((2 * STAGES + 1,)),
             sem((4,)), sem((4,)), sem((4,)), sem((4,)),
             sem((4,)), sem((4,)), sem((4,)), sem((4,)),
             sem((4,)), sem((4,)), sem((1,)), sem((1,)),
@@ -301,6 +329,15 @@
         ),
         cost_estimate=pl.CostEstimate(flops=2 << 30, bytes_accessed=4 << 20, transcendentals=0),
     )(tokens, w_gate, w_up, w_down, upstream)
+    results = [pltpu.with_memory_space_constraint(r, pltpu.VMEM) for r in results]
+    return pl.pallas_call(
+        write_out,
+        name="write_out",
+        out_shape=tuple(jax.ShapeDtypeStruct(shape, bf16) for shape in shapes),
+        in_specs=[pl.BlockSpec(memory_space=pltpu.VMEM)] * 4,
+        out_specs=(pl.BlockSpec(memory_space=pltpu.HBM),) * 4,
+        scratch_shapes=[sem((4,))],
+    )(*results)
 
 
 def solution(mesh):

time: 76.1 us -> 65.2 us (0.86)
  local copies, waits for them, and re-layouts: 5.28 us -> 0 us
  Pallas kernels: 69.5 us -> 64.4 us
    unnamed x8 -> x0, local copies, waits for them, and re-layouts: 5.28 us -> none
    pallas_call x1 -> x2, Pallas kernels: 69.5 us -> 64.4 us  [the longest x1 63.2 us: body(): pl.pallas_call(kernel, name='mlp', out_shape=tuple((pltpu.VMEM(shape, bf1...]
where the time goes in v2:
time: 65.2 us; the launch traced here: 65.1 us
  Pallas kernels  64.4 us (99%)
    pallas_call x1, Pallas kernels, body(): pl.pallas_call(kernel, name='mlp', out_shape=tuple((pltpu.VMEM(shape, bf1...  63.2 us

profile of v2, /device:TPU:1, one launch (start us, length us, event | category | flops | bytes accessed | tf_op | source)
XLA Modules:
  0.0 65.1 jit_solution(676325680514920078)
XLA Ops:
  0.6 63.2 %mlp.1 = (bf16[16,512]{1,0:T(8,128)(2,1)S(1)}, bf16[512,512]{1,0:T(8,128)(2,1)S(1)}, bf16[512,512]{1,0:T(8,128)(2,1)S(1)}, bf16[512,512]{1,0:T(8,128)(2,1)S(1)}) custom-call(bf16[16,512]{1,0:T(8,128)(2,1)} %tokens_ref.1, bf16[512,512]{1,0:T(8,128)(2,1)} %wg_ref.1, bf16[512,512]{1,0:T(8,128)(2,1)} %wu_ref.1, bf16[512,512]{1,0:T(8,128)(2,1)} %wd_ref.1, ...), custom_call_target="tpu_custom_call" | custom-call | flops 2147483648 | bytes 4194304 | tf_op jit(solution)/shard_map/mlp/pallas_call | solution.py:302
  63.9 1.2 %write_out.1 = (bf16[16,512]{1,0:T(8,128)(2,1)}, bf16[512,512]{1,0:T(8,128)(2,1)}, bf16[512,512]{1,0:T(8,128)(2,1)}, bf16[512,512]{1,0:T(8,128)(2,1)}) custom-call(bf16[16,512]{1,0:T(8,128)(2,1)S(1)} %get-tuple-element.8.refs_0_, bf16[512,512]{1,0:T(8,128)(2,1)S(1)} %get-tuple-element.9.refs_1_, bf16[512,512]{1,0:T(8,128)(2,1)S(1)} %get-tuple-element.10.refs_2_, ...), custom_call_target="tpu_custom_call" | custom-call | tf_op jit(solution)/shard_map/write_out/pallas_call | solution.py:333

commit v3 on v2

--- a/solution.py
+++ b/solution.py
@@ -10,13 +10,14 @@
 CHUNKS = 4
 ROWS = 128
 B = 16
-ORDER = [0, 1, -1, 2, -2, 3, -3, 4, -4, 5, -5, 6, -6, 7, -7, 8]
+ORDER = [0, 1, -1, 2, 3, -3, 4, -4, 5, -5, 6, -6, -2, 7, -7, 8]
 SLOT = {r: s for s, r in enumerate(ORDER)}
 SLOT[-8] = SLOT[8]
 REACH = (3, 3, 2)
 BASE = [sum(REACH[:s]) for s in range(len(REACH) + 1)]
 STAGES = len(REACH)
 
+LAST = (0, 2, 1, 3)
 SCHEDULE = (
     ("relay", 0),
     ("nearer", 0),
@@ -24,30 +25,30 @@
     ("relay", 1),
     ("nearer", 1),
     ("project", 2),
-    ("project", 1),
     ("relay", 2),
     ("nearer", 2),
+    ("add", 0),
+    ("project", 3),
     ("add", 2),
-    ("project", 3),
+    ("project", 1),
+    ("add", 3),
     ("activate", 2),
+    ("activate", 0),
     ("add", 1),
-    ("add", 3),
+    ("activate", 3),
     ("spread", 2),
-    ("activate", 3),
-    ("add", 0),
+    ("spread", 3),
     ("activate", 1),
     ("product", 2),
-    ("spread", 3),
     ("send", 2),
-    ("activate", 0),
+    ("spread", 0),
     ("product", 3),
+    ("send", 3),
     ("spread", 1),
-    ("spread", 0),
-    ("send", 3),
+    ("product", 0),
+    ("send", 0),
     ("product", 1),
     ("send", 1),
-    ("product", 0),
-    ("send", 0),
 )
 
 
@@ -175,8 +176,8 @@
                 p = contract_last(ups, weights[2])
             part[c, i] = p
             part16[c, i] = p.astype(jnp.bfloat16)
-        for h, (first, at, _, _) in enumerate(halves):
-            for d in (1, 2, 3):
+        for d in (2, 1, 3):
+            for h, (first, at, _, _) in enumerate(halves):
                 b = lax.rem(at + d, 4)
                 block = pl.ds(pl.multiple_of(h * 64 + b * B, B), B)
                 put(
@@ -191,7 +192,8 @@
             for d in range(3):
                 total = total + got1[c, h, d].astype(jnp.float32)
             sum1[c, h] = total
-            for d in (1, 2, 3):
+        for d in (2, 1, 3):
+            for h, (_, _, second, place) in enumerate(halves):
                 j = lax.rem(place + d, 4)
                 cols = pl.ds(pl.multiple_of(j * 128, 128), 128)
                 put(
@@ -216,16 +218,18 @@
             hidden[0, rows, cols] = (activated * up).astype(jnp.bfloat16)
             hidden[1, rows, cols] = (slope * up * s * (1.0 + gate * (1.0 - s))).astype(jnp.bfloat16)
             hidden[2, rows, cols] = (slope * activated).astype(jnp.bfloat16)
-            block = hidden.at[:, rows, cols]
-            for d in (1, 2, 3):
+        for d in (2, 1, 3):
+            for h, (_, at, second, place) in enumerate(halves):
+                rows, cols = own(c, h, at, place)
+                block = hidden.at[:, rows, cols]
                 put(block, block, c1_send.at[c], c1_recv.at[c], second(d))
 
     def spread(c):
         take(hidden.at[:, 0:96, 0:128], c1_recv.at[c])
-        for h, (first, at, _, place) in enumerate(halves):
-            rows, _ = own(c, h, at, place)
-            block = hidden.at[:, rows, :]
-            for d in (1, 2, 3):
+        for d in (2, 1, 3):
+            for h, (first, at, _, place) in enumerate(halves):
+                rows, _ = own(c, h, at, place)
+                block = hidden.at[:, rows, :]
                 put(block, block, c2_send.at[c], c2_recv.at[c], first(d))
 
     def input_part(c):
@@ -237,14 +241,14 @@
 
     def input_send(c):
         take(inp_got.at[c], e_recv.at[c])
-        for i in range(4):
+        for i in reversed(range(4)):
             slot = 4 * c + i
             total = inp[c, i, core] + inp_got[c, i]
             if slot == 0:
                 inp_got[c, i] = total
             else:
                 inp16[c, i] = total.astype(jnp.bfloat16)
-                put(inp16.at[c, i], inp_all.at[slot - 1], d_send.at[0], d_recv.at[0], along_z(ORDER[slot]))
+                put(inp16.at[c, i], inp_all.at[slot - 1], d_send.at[0], d_recv.at[c], along_z(ORDER[slot]))
 
     def weight_grads():
         pairs = ((acts, 0, hidden, 1, gg_ref), (acts, 0, hidden, 2, gu_ref), (hidden, 0, acts, 1, gd_ref))
@@ -266,12 +270,6 @@
         tasks[name](c)
     weight_grads()
 
-    take(inp_all, d_recv.at[0])
-    total = inp_got[0, 0]
-    for i in range(15):
-        total = total + inp_all[i].astype(jnp.float32)
-    gt_ref[...] = total.astype(jnp.bfloat16)
-
     for group, rels in enumerate(groups):
         if rels:
             take(few(len(rels)), a_send.at[group])
@@ -283,6 +281,14 @@
         take(hidden.at[:, 0:96, 0:128], c1_send.at[c])
         take(hidden.at[:, 0:96, :], c2_send.at[c])
         take(inp_got.at[c], e_send.at[c])
+
+    total = inp_got[0, 0]
+    for c in LAST:
+        slots = range(max(4 * c, 1), 4 * c + 4)
+        take(inp_all.at[slots[0] - 1 : slots[-1]], d_recv.at[c])
+        for slot in slots:
+            total = total + inp_all[slot - 1].astype(jnp.float32)
+    gt_ref[...] = total.astype(jnp.bfloat16)
     take(inp_all, d_send.at[0])
 
 
@@ -322,7 +328,7 @@
             sem((2 * STAGES,)), sem((2 * STAGES,)), sem((2 * STAGES + 1,)), sem((2 * STAGES + 1,)),
             sem((4,)), sem((4,)), sem((4,)), sem((4,)),
             sem((4,)), sem((4,)), sem((4,)), sem((4,)),
-            sem((4,)), sem((4,)), sem((1,)), sem((1,)),
+            sem((4,)), sem((4,)), sem((1,)), sem((4,)),
         ],
         compiler_params=pltpu.CompilerParams(
             collective_id=0, has_side_effects=True, vmem_limit_bytes=60 << 20

time: 65.2 us -> 63.9 us (0.980)
  Pallas kernels: 64.4 us -> 63 us
    pallas_call x1, Pallas kernels: 63.2 us -> 61.9 us  [body(): pl.pallas_call(kernel, name='mlp', out_shape=tuple((pltpu.VMEM(shape, bf1...]
where the time goes in v3:
time: 63.9 us; the launch traced here: 63.7 us
  Pallas kernels  63 us (99%)
  between operations  0.64 us (1%)
    pallas_call x1, Pallas kernels, body(): pl.pallas_call(kernel, name='mlp', out_shape=tuple((pltpu.VMEM(shape, bf1...  61.9 us

profile of v3, /device:TPU:1, one launch (start us, length us, event | category | flops | bytes accessed | tf_op | source)
XLA Modules:
  0.0 63.7 jit_solution(10111492546291597293)
XLA Ops:
  0.6 61.9 %mlp.1 = (bf16[16,512]{1,0:T(8,128)(2,1)S(1)}, bf16[512,512]{1,0:T(8,128)(2,1)S(1)}, bf16[512,512]{1,0:T(8,128)(2,1)S(1)}, bf16[512,512]{1,0:T(8,128)(2,1)S(1)}) custom-call(bf16[16,512]{1,0:T(8,128)(2,1)} %tokens_ref.1, bf16[512,512]{1,0:T(8,128)(2,1)} %wg_ref.1, bf16[512,512]{1,0:T(8,128)(2,1)} %wu_ref.1, bf16[512,512]{1,0:T(8,128)(2,1)} %wd_ref.1, ...), custom_call_target="tpu_custom_call" | custom-call | flops 2147483648 | bytes 4194304 | tf_op jit(solution)/shard_map/mlp/pallas_call | solution.py:308
  62.5 1.2 %write_out.1 = (bf16[16,512]{1,0:T(8,128)(2,1)}, bf16[512,512]{1,0:T(8,128)(2,1)}, bf16[512,512]{1,0:T(8,128)(2,1)}, bf16[512,512]{1,0:T(8,128)(2,1)}) custom-call(bf16[16,512]{1,0:T(8,128)(2,1)S(1)} %get-tuple-element.8.refs_0_, bf16[512,512]{1,0:T(8,128)(2,1)S(1)} %get-tuple-element.9.refs_1_, bf16[512,512]{1,0:T(8,128)(2,1)S(1)} %get-tuple-element.10.refs_2_, ...), custom_call_target="tpu_custom_call" | custom-call | tf_op jit(solution)/shard_map/write_out/pallas_call | solution.py:339

commit v4 on v3

--- a/solution.py
+++ b/solution.py
@@ -52,12 +52,6 @@
 )
 
 
-def contract_last(left, right):
-    return lax.dot_general(
-        left, right, (((1,), (1,)), ((), ())), preferred_element_type=jnp.float32
-    )
-
-
 def contract_first(left, right):
     return lax.dot_general(
         left, right, (((0,), (0,)), ((), ())), preferred_element_type=jnp.float32
@@ -67,7 +61,7 @@
 def kernel(
     tokens_ref, wg_ref, wu_ref, wd_ref, upstream_ref,
     gt_ref, gg_ref, gu_ref, gd_ref,
-    acts, weights, part, part16, got1, sum1, got2, hidden, inp, inp_got, inp16, inp_all,
+    acts, weights, turned, part, part16, got1, sum1, got2, hidden, inp, inp_got, inp16, inp_all,
     in_sem, a_send, a_recv, k_send, k_recv, b1_send, b1_recv, b2_send, b2_recv,
     c1_send, c1_recv, c2_send, c2_recv, e_send, e_recv, d_send, d_recv,
 ):
@@ -99,6 +93,11 @@
     def shard(slot, c):
         return acts.at[:, pl.ds(pl.multiple_of(slot * 2 * B + c * B, B), B), :]
 
+    barrier = pltpu.get_barrier_semaphore()
+    greet = [along_z(sign * d) for d in range(1, max(REACH) + 1) for sign in (1, -1)] + [sibling]
+    greet += [along_x(d) for d in (1, 2, 3)] + [along_y(d) for d in (1, 2, 3)]
+    for peer in greet:
+        pl.semaphore_signal(barrier, inc=1, device_id=peer, device_id_type=MESH)
     mine = pl.ds(pl.multiple_of(core * B, B), B)
     loads = [
         pltpu.make_async_copy(tokens_ref, acts.at[0, mine, :], in_sem.at[0]),
@@ -109,12 +108,6 @@
     ]
     for load in loads:
         load.start()
-
-    barrier = pltpu.get_barrier_semaphore()
-    greet = [along_z(sign * d) for d in range(1, max(REACH) + 1) for sign in (1, -1)] + [sibling]
-    greet += [along_x(d) for d in (1, 2, 3)] + [along_y(d) for d in (1, 2, 3)]
-    for peer in greet:
-        pl.semaphore_signal(barrier, inc=1, device_id=peer, device_id_type=MESH)
     loads[0].wait()
     loads[1].wait()
     pl.semaphore_wait(barrier, len(greet))
@@ -173,7 +166,7 @@
             if i < 2:
                 p = jnp.dot(tok, weights[i], preferred_element_type=jnp.float32)
             else:
-                p = contract_last(ups, weights[2])
+                p = jnp.dot(ups, turned[2], preferred_element_type=jnp.float32)
             part[c, i] = p
             part16[c, i] = p.astype(jnp.bfloat16)
         for d in (2, 1, 3):
@@ -235,7 +228,8 @@
     def input_part(c):
         take(hidden.at[:, 0:96, :], c2_recv.at[c])
         rows = slice(c * ROWS, (c + 1) * ROWS)
-        p = contract_last(hidden[1, rows, :], weights[0]) + contract_last(hidden[2, rows, :], weights[1])
+        p = jnp.dot(hidden[1, rows, :], turned[0], preferred_element_type=jnp.float32)
+        p = p + jnp.dot(hidden[2, rows, :], turned[1], preferred_element_type=jnp.float32)
         inp[c] = p.reshape(4, 2, B, 512)
         put(inp.at[c, :, 1 - core], inp_got.at[c], e_send.at[c], e_recv.at[c], sibling)
 
@@ -257,16 +251,15 @@
 
     gather_send(0)
     to_sibling((0,), 2 * STAGES)
-    loaded = False
+    for load in loads[2:]:
+        load.wait()
+    for i in range(3):
+        turned[i] = weights[i].T
     tasks = dict(
         relay=relay, nearer=nearer, project=project, add=add_first, activate=activate, spread=spread,
         product=input_part, send=input_send,
     )
     for name, c in SCHEDULE:
-        if name == "project" and not loaded:
-            for load in loads[2:]:
-                load.wait()
-            loaded = True
         tasks[name](c)
     weight_grads()
 
@@ -313,6 +306,7 @@
         out_specs=(pl.BlockSpec(memory_space=pltpu.VMEM),) * 4,
         scratch_shapes=[
             pltpu.VMEM((2, 512, 512), bf16),
+            pltpu.VMEM((3, 512, 512), bf16),
             pltpu.VMEM((3, 512, 512), bf16),
             pltpu.VMEM((CHUNKS, 3, ROWS, 512), f32),
             pltpu.VMEM((CHUNKS, 3, ROWS, 512), bf16),

time: 63.9 us -> 63.6 us (level)
  no operation moved by 1% of the time
where the time goes in v4:
time: 63.6 us; the launch traced here: 63.2 us
  Pallas kernels  62.6 us (98%)
  between operations  0.64 us (1%)
    pallas_call x1, Pallas kernels, body(): pl.pallas_call(kernel, name='mlp', out_shape=tuple((pltpu.VMEM(shape, bf1...  61.4 us

profile of v4, /device:TPU:1, one launch (start us, length us, event | category | flops | bytes accessed | tf_op | source)
XLA Modules:
  0.0 63.2 jit_solution(4084597727152116674)
XLA Ops:
  0.6 61.4 %mlp.1 = (bf16[16,512]{1,0:T(8,128)(2,1)S(1)}, bf16[512,512]{1,0:T(8,128)(2,1)S(1)}, bf16[512,512]{1,0:T(8,128)(2,1)S(1)}, bf16[512,512]{1,0:T(8,128)(2,1)S(1)}) custom-call(bf16[16,512]{1,0:T(8,128)(2,1)} %tokens_ref.1, bf16[512,512]{1,0:T(8,128)(2,1)} %wg_ref.1, bf16[512,512]{1,0:T(8,128)(2,1)} %wu_ref.1, bf16[512,512]{1,0:T(8,128)(2,1)} %wd_ref.1, ...), custom_call_target="tpu_custom_call" | custom-call | flops 2147483648 | bytes 4194304 | tf_op jit(solution)/shard_map/mlp/pallas_call | solution.py:301
  62.0 1.2 %write_out.1 = (bf16[16,512]{1,0:T(8,128)(2,1)}, bf16[512,512]{1,0:T(8,128)(2,1)}, bf16[512,512]{1,0:T(8,128)(2,1)}, bf16[512,512]{1,0:T(8,128)(2,1)}) custom-call(bf16[16,512]{1,0:T(8,128)(2,1)S(1)} %get-tuple-element.8.refs_0_, bf16[512,512]{1,0:T(8,128)(2,1)S(1)} %get-tuple-element.9.refs_1_, bf16[512,512]{1,0:T(8,128)(2,1)S(1)} %get-tuple-element.10.refs_2_, ...), custom_call_target="tpu_custom_call" | custom-call | tf_op jit(solution)/shard_map/write_out/pallas_call | solution.py:333

commit v5 on v4

--- a/solution.py
+++ b/solution.py
@@ -17,7 +17,7 @@
 BASE = [sum(REACH[:s]) for s in range(len(REACH) + 1)]
 STAGES = len(REACH)
 
-LAST = (0, 2, 1, 3)
+LAST = (0, 2, 3, 1)
 SCHEDULE = (
     ("relay", 0),
     ("nearer", 0),

time: 63.6 us -> 63.6 us (level)
  no operation moved by 1% of the time
where the time goes in v5:
time: 63.6 us; the launch traced here: 63.2 us
  Pallas kernels  62.6 us (98%)
  between operations  0.64 us (1%)
    pallas_call x1, Pallas kernels, body(): pl.pallas_call(kernel, name='mlp', out_shape=tuple((pltpu.VMEM(shape, bf1...  61.4 us

profile of v5, /device:TPU:1, one launch (start us, length us, event | category | flops | bytes accessed | tf_op | source)
XLA Modules:
  0.0 63.2 jit_solution(3105969676742815117)
XLA Ops:
  0.6 61.4 %mlp.1 = (bf16[16,512]{1,0:T(8,128)(2,1)S(1)}, bf16[512,512]{1,0:T(8,128)(2,1)S(1)}, bf16[512,512]{1,0:T(8,128)(2,1)S(1)}, bf16[512,512]{1,0:T(8,128)(2,1)S(1)}) custom-call(bf16[16,512]{1,0:T(8,128)(2,1)} %tokens_ref.1, bf16[512,512]{1,0:T(8,128)(2,1)} %wg_ref.1, bf16[512,512]{1,0:T(8,128)(2,1)} %wu_ref.1, bf16[512,512]{1,0:T(8,128)(2,1)} %wd_ref.1, ...), custom_call_target="tpu_custom_call" | custom-call | flops 2147483648 | bytes 4194304 | tf_op jit(solution)/shard_map/mlp/pallas_call | solution.py:301
  62.0 1.2 %write_out.1 = (bf16[16,512]{1,0:T(8,128)(2,1)}, bf16[512,512]{1,0:T(8,128)(2,1)}, bf16[512,512]{1,0:T(8,128)(2,1)}, bf16[512,512]{1,0:T(8,128)(2,1)}) custom-call(bf16[16,512]{1,0:T(8,128)(2,1)S(1)} %get-tuple-element.8.refs_0_, bf16[512,512]{1,0:T(8,128)(2,1)S(1)} %get-tuple-element.9.refs_1_, bf16[512,512]{1,0:T(8,128)(2,1)S(1)} %get-tuple-element.10.refs_2_, ...), custom_call_target="tpu_custom_call" | custom-call | tf_op jit(solution)/shard_map/write_out/pallas_call | solution.py:333
